TPU v7x, 32 devices: a whole 2x2x4 slice. The times are simulated.
32 devices in a mesh: blocks: 2 (over x), strip: 16 (over z, y, core).
Axes of the slice: x: 2, y: 2, z: 4, core: 2. Of those that a mesh axis runs over, the one named last changes fastest.
Arguments:
- estimate: float32 [128, 256, 256], P(('blocks', 'strip')), parts along dimension 0, may hold values from 0.5 to 2
- views_data: bfloat16 [8, 128, 256, 256], P(None, ('blocks', 'strip')), parts along dimension 1, may hold values from 0.02 to 30, as said below
- kernel_x: float32 [8, 9], replicated, may hold values from 0.1 to 1
- kernel_y: float32 [8, 5], replicated, may hold values from 0.1 to 1
- kernel_z: float32 [8, 9], replicated, may hold values from 0.1 to 1
Outputs:
- deconvolved: float32 [128, 256, 256], P(('blocks', 'strip')), parts along dimension 0
There are 2 independent parts, one for each index of `blocks`. A program takes and returns all parts, laid end to end along the dimension named above; an argument that names none is the same for every part. Nothing has to cross between parts.
Inputs may be any that keep to these rules, and one draw needn't show every extreme that they name: `views_data`: positive recorded intensities of each view.
All inputs are finite; a program needn't handle non-finite values.
Results may differ from a plain program's by a relative error of at most 0.00067.
Values may be sent and summed in bfloat16 or wider, within the bound.
A program may use at most 128 MiB of HBM per device.

v0:
```python
import functools

import jax
import jax.numpy as jnp
from jax import lax
from jax.experimental import pallas as pl
from jax.experimental.pallas import tpu as pltpu
from jax.sharding import PartitionSpec as P

ITERS = 2
CHUNK = 16
MESH = pl.DeviceIdType.MESH
BF = jnp.bfloat16
F32 = jnp.float32


def band(taps_ref, view, length, radius, start, size, flip):
    rows = lax.broadcasted_iota(jnp.int32, (size, length), 0) + start
    columns = lax.broadcasted_iota(jnp.int32, (size, length), 1)
    place = (rows - columns if flip else columns - rows) + radius
    total = jnp.zeros((size, length), F32)
    for t in range(2 * radius + 1):
        total = jnp.where(place == t, taps_ref[view, t], total)
    return total.astype(BF)


def along_y(rows, taps, mirror):
    width = len(taps)
    outs = []
    for o in range(len(rows) - width + 1):
        terms = [
            taps[width - 1 - t if mirror else t] * rows[o + t] for t in range(width)
        ]
        while len(terms) > 1:
            terms = [a + b for a, b in zip(terms[::2], terms[1::2])] + (
                terms[-1:] if len(terms) % 2 else []
            )
        outs.append(terms[0])
    return outs


def dot(a, b):
    return jnp.dot(a, b, preferred_element_type=F32)


def kernel(
    strips, nx, ny, nz, est, data, out,
    img, wide, ax, axt, bz, bzt, fy, ratio, acc,
    local_sem, img_send, img_recv, data_send, data_recv,
):
    views, own, length_x, length_z = data.shape
    ry = (ny.shape[1] - 1) // 2
    rx = (nx.shape[1] - 1) // 2
    rz = (nz.shape[1] - 1) // 2
    halo = 2 * ry
    inner = own + 2 * ry
    me = lax.axis_index("strip")
    has = (me > 0, me < strips - 1)
    peer = (me - 1, me + 1)

    barrier = pltpu.get_barrier_semaphore()
    for side in range(2):
        @pl.when(has[side])
        def _():
            pl.semaphore_signal(
                barrier, inc=1, device_id={"strip": peer[side]}, device_id_type=MESH
            )

    fetch = pltpu.make_async_copy(data, wide.at[:, ry : ry + own], local_sem)
    fetch.start()
    img[0, halo : halo + own] = est[...].astype(BF)
    for side in range(2):
        at_image = slice(0, halo) if side == 0 else slice(halo + own, 2 * halo + own)
        at_data = slice(0, ry) if side == 0 else slice(ry + own, 2 * ry + own)

        @pl.when(jnp.logical_not(has[side]))
        def _():
            for step in range(ITERS):
                img[step, at_image] = jnp.zeros((halo, length_x, length_z), BF)
            wide[:, at_data] = jnp.zeros((views, ry, length_x, length_z), BF)

    def image_copy(step, side):
        if side == 0:
            source, target = pl.ds(halo, halo), pl.ds(halo + own, halo)
        else:
            source, target = pl.ds(own, halo), pl.ds(0, halo)
        return pltpu.make_async_remote_copy(
            src_ref=img.at[step, source],
            dst_ref=img.at[step, target],
            send_sem=img_send.at[step, side],
            recv_sem=img_recv.at[step, 1 - side],
            device_id={"strip": peer[side]},
            device_id_type=MESH,
        )

    def data_copy(view, side):
        if side == 0:
            source, target = pl.ds(0, ry), pl.ds(ry + own, ry)
        else:
            source, target = pl.ds(own - ry, ry), pl.ds(0, ry)
        return pltpu.make_async_remote_copy(
            src_ref=data.at[view, source],
            dst_ref=wide.at[view, target],
            send_sem=data_send.at[side, view],
            recv_sem=data_recv.at[1 - side, view],
            device_id={"strip": peer[side]},
            device_id_type=MESH,
        )

    pl.semaphore_wait(
        barrier, jnp.where(has[0], 1, 0) + jnp.where(has[1], 1, 0)
    )
    for side in range(2):
        @pl.when(has[side])
        def _():
            image_copy(0, side).start()

    @pl.loop(0, views)
    def _(view):
        for side in range(2):
            @pl.when(has[side])
            def _():
                data_copy(view, side).start()

    @pl.loop(0, views)
    def _(view):
        for chunk in range(0, length_x, 64):
            at = pl.ds(chunk, 64)
            ax[view, at] = band(nx, view, length_x, rx, chunk, 64, False)
            axt[view, at] = band(nx, view, length_x, rx, chunk, 64, True)
        for chunk in range(0, length_z, 64):
            at = pl.ds(chunk, 64)
            bz[view, at] = band(nz, view, length_z, rz, chunk, 64, True)
            bzt[view, at] = band(nz, view, length_z, rz, chunk, 64, False)

    fetch.wait()

    for step in range(ITERS):
        for side in range(2):
            @pl.when(has[side])
            def _():
                image_copy(step, 1 - side).wait_recv()

        acc[...] = jnp.zeros_like(acc)

        @pl.loop(0, views)
        def _(view):
            taps = [
                jnp.full((CHUNK, length_z), ny[view, t], F32).astype(BF)
                for t in range(2 * ry + 1)
            ]

            @pl.loop(0, length_x // CHUNK, unroll=2)
            def _(chunk):
                at = pl.ds(pl.multiple_of(chunk * CHUNK, CHUNK), CHUNK)
                rows = [img[step, j, at, :] for j in range(own + 2 * halo)]
                for o, value in enumerate(along_y(rows, taps, False)):
                    fy[o, at, :] = value

            if step == 0:
                for side in range(2):
                    @pl.when(has[side])
                    def _():
                        data_copy(view, 1 - side).wait_recv()

            for o in range(inner):
                second = dot(ax[view], fy[o]).astype(BF)
                blurred = dot(second, bz[view])
                ratio[o] = wide[view, o] * pl.reciprocal(blurred, approx=True).astype(BF)

            @pl.loop(0, length_x // CHUNK, unroll=2)
            def _(chunk):
                at = pl.ds(pl.multiple_of(chunk * CHUNK, CHUNK), CHUNK)
                rows = [ratio[j, at, :] for j in range(inner)]
                for o, value in enumerate(along_y(rows, taps, True)):
                    fy[o, at, :] = value

            for o in range(own):
                second = dot(axt[view], fy[o]).astype(BF)
                acc[o] += jnp.log(dot(second, bzt[view]))

        before = est if step == 0 else out
        out[...] = before[...] * jnp.exp(acc[...] * (1.0 / views))
        if step < ITERS - 1:
            img[step + 1, halo : halo + own] = out[...].astype(BF)
            for side in range(2):
                @pl.when(has[side])
                def _():
                    image_copy(step + 1, side).start()

    for side in range(2):
        @pl.when(has[side])
        def _():
            for step in range(ITERS):
                image_copy(step, side).wait_send()

            @pl.loop(0, views)
            def _(view):
                data_copy(view, side).wait_send()


def local(strips, estimate, views_data, kernel_x, kernel_y, kernel_z):
    views, own, length_x, length_z = views_data.shape
    norm_x, norm_y, norm_z = (
        k / jnp.sum(k, axis=1, keepdims=True) for k in (kernel_x, kernel_y, kernel_z)
    )
    ry = (kernel_y.shape[1] - 1) // 2
    inner = own + 2 * ry
    smem = pl.BlockSpec(memory_space=pltpu.SMEM)
    vmem = pl.BlockSpec(memory_space=pltpu.VMEM)
    plane = (length_x, length_z)
    flops = ITERS * views * (inner + own) * 2 * length_x * length_z * (length_x + length_z)
    unweighted = pl.pallas_call(
        functools.partial(kernel, strips),
        out_shape=jax.ShapeDtypeStruct(estimate.shape, F32),
        in_specs=[smem, smem, smem, vmem, pl.BlockSpec(memory_space=pl.ANY)],
        out_specs=vmem,
        scratch_shapes=[
            pltpu.VMEM((ITERS, own + 4 * ry) + plane, BF),
            pltpu.VMEM((views, inner) + plane, BF),
            pltpu.VMEM((views, length_x, length_x), BF),
            pltpu.VMEM((views, length_x, length_x), BF),
            pltpu.VMEM((views, length_z, length_z), BF),
            pltpu.VMEM((views, length_z, length_z), BF),
            pltpu.VMEM((inner,) + plane, BF),
            pltpu.VMEM((inner,) + plane, BF),
            pltpu.VMEM((own,) + plane, F32),
            pltpu.SemaphoreType.DMA,
            pltpu.SemaphoreType.DMA((ITERS, 2)),
            pltpu.SemaphoreType.DMA((ITERS, 2)),
            pltpu.SemaphoreType.DMA((2, views)),
            pltpu.SemaphoreType.DMA((2, views)),
        ],
        compiler_params=pltpu.CompilerParams(
            collective_id=0, has_side_effects=True, vmem_limit_bytes=44 * 1024 * 1024
        ),
        cost_estimate=pl.CostEstimate(
            flops=flops, bytes_accessed=8 * 1024 * 1024, transcendentals=0
        ),
    )(norm_x, norm_y, norm_z, estimate, views_data)
    totals = lax.psum(jnp.sum(views_data, axis=(1, 2, 3), dtype=F32), "strip")
    log_weights = jnp.log(jnp.sum(totals) / (views * totals))
    return unweighted * jnp.exp(jnp.sum(log_weights) / views)


def solution(mesh):
    placed = (
        P(("blocks", "strip"), None, None),
        P(None, ("blocks", "strip"), None, None),
        P(),
        P(),
        P(),
    )
    return jax.shard_map(
        functools.partial(local, mesh.shape["strip"]),
        mesh=mesh,
        in_specs=placed,
        out_specs=P(("blocks", "strip"), None, None),
        check_vma=False,
    )
```

profile of v0, /device:TPU:1, one launch (start us, length us, event | category | flops | bytes accessed | tf_op | source)
XLA Modules:
  0.0 133.1 jit_solution(1475639852966225812)
XLA Ops:
  0.0 0.8 reduce_sum.54
  0.8 0.8 reduce_sum.56
  1.6 0.8 broadcast_divide_fusion
  2.4 0.8 reduce_sum.55
  3.2 0.8 broadcast_divide_fusion.1.ny
  4.0 0.0 copy-start
  4.0 2.2 %copy-done = bf16[8,4,256,256]{3,2,1,0:T(8,128)(2,1)S(1)} copy-done((bf16[8,4,256,256]{3,2,1,0:T(8,128)(2,1)S(1)}, bf16[8,4,256,256]{3,2,1,0:T(8,128)(2,1)}, u32[]{:S(2)}) %copy-start) | copy-done | bytes 4194328
  6.1 0.0 copy-start.1
  6.1 1.2 copy-done.1
  7.4 92.9 %shard_map.55 = f32[4,256,256]{2,1,0:T(8,128)S(1)} custom-call(f32[8,9]{1,0:T(8,128)S(1)} %get-tuple-element.6.nx, f32[8,5]{1,0:T(8,128)S(1)} %broadcast_divide_fusion.1.ny, f32[8,9]{1,0:T(8,128)S(1)} %get-tuple-element.5.nz, f32[4,256,256]{2,1,0:T(8,128)S(1)} %copy-done.1, bf16[8,4,256,256]{3,2,1,0:T(8,128)(2,1)S(1)} %copy-done), custom_call_target="tpu_custom_call" | custom-call | flops 12884901888 | bytes 8388608 | tf_op jit(solution)/shard_map/pallas_call | solution.py:213
  100.3 0.8 convert_reduce_fusion
  101.0 28.3 %psum.7 = f32[8]{0:T(128)S(1)} all-reduce(f32[8]{0:T(128)S(1)} %convert_reduce_fusion), channel_id=1, replica_groups=mesh['blocks'=2,'strip'=16] {'strip'}, use_global_device_ids=true, to_apply=%region_4.0 | all-reduce | flops 8 | bytes 64 | tf_op jit(solution)/shard_map/psum | solution.py:241
  129.3 0.6 reduce_sum.58
  129.9 1.3 %log_reduce_fusion = f32[]{:T(128)} fusion(f32[8]{0:T(128)S(1)} %psum.7, f32[]{:T(128)} %reduce_sum.58), kind=kLoop, calls=%fused_computation.5 | loop fusion | flops 23 | bytes 40 | tf_op jit(solution)/shard_map/reduce_sum | solution.py:243
  132.0 1.1 broadcast_multiply_fusion
Async XLA Ops:
  4.0 2.2 %copy-start = (bf16[8,4,256,256]{3,2,1,0:T(8,128)(2,1)S(1)}, bf16[8,4,256,256]{3,2,1,0:T(8,128)(2,1)}, u32[]{:S(2)}) copy-start(bf16[8,4,256,256]{3,2,1,0:T(8,128)(2,1)} %data.1) | copy-start | bytes 12582916
  6.1 1.2 copy-start.1
where the time goes:
time: 135 us; the launch traced here: 133 us
  Pallas kernels  92.9 us (69%)
  blocking collectives  28.3 us (21%)
  other arithmetic  7.72 us (6%)
  local copies, waits for them, and re-layouts  3.42 us (3%)
    pallas_call x1, Pallas kernels, local(): pl.pallas_call(functools.partial(kernel, strips), out_shape=jax.ShapeDtyp...  92.9 us
    psum x1, blocking collectives, local(): totals = lax.psum(jnp.sum(views_data, axis=(1, 2, 3), dtype=F32), 'strip')  28.3 us
    unnamed x4, local copies, waits for them, and re-layouts  3.42 us

commit v1 on v0

v1 whole, which is shorter than its diff:
```python
import functools

import jax
import jax.numpy as jnp
from jax import lax
from jax.experimental import pallas as pl
from jax.experimental.pallas import tpu as pltpu
from jax.sharding import PartitionSpec as P

ITERS = 2
CHUNK = 16
BLOCK = 64
AHEAD = 2
MESH = pl.DeviceIdType.MESH
BF = jnp.bfloat16
F32 = jnp.float32
KINDS = (F32, BF)


def normalised(taps_ref, view):
    taps = [taps_ref[view, t] for t in range(taps_ref.shape[1])]
    total = taps[0]
    for tap in taps[1:]:
        total = total + tap
    return [tap / total for tap in taps]


def band(taps, length, radius, start, size, flip):
    rows = lax.broadcasted_iota(jnp.int32, (size, length), 0) + start
    columns = lax.broadcasted_iota(jnp.int32, (size, length), 1)
    place = (rows - columns if flip else columns - rows) + radius
    total = jnp.zeros((size, length), F32)
    for t in range(2 * radius + 1):
        total = jnp.where(place == t, taps[t], total)
    return total.astype(BF)


def along_y(rows, taps, mirror):
    width = len(taps)
    outs = []
    for o in range(len(rows) - width + 1):
        terms = [
            taps[width - 1 - t if mirror else t] * rows[o + t] for t in range(width)
        ]
        while len(terms) > 1:
            terms = [a + b for a, b in zip(terms[::2], terms[1::2])] + (
                terms[-1:] if len(terms) % 2 else []
            )
        outs.append(terms[0])
    return outs


def dot(a, b):
    return jnp.dot(a, b, preferred_element_type=F32)


def kernel(
    strips, nx, ny, nz, est, data, out,
    img, wide, ax, axt, bz, bzt, half, ratio, acc, first, mine, parts,
    local_sem, est_sem, img_send, img_recv, data_send, data_recv, sum_send, sum_recv,
):
    views, own, length_x, length_z = data.shape
    ry = (ny.shape[1] - 1) // 2
    rx = (nx.shape[1] - 1) // 2
    rz = (nz.shape[1] - 1) // 2
    halo = 2 * ry
    inner = own + 2 * ry
    me = lax.axis_index("strip")
    has = (me > 0, me < strips - 1)
    peer = (me - 1, me + 1)

    fetch_first = pltpu.make_async_copy(est, first, est_sem)
    fetch_first.start()
    barrier = pltpu.get_barrier_semaphore()

    @pl.loop(1, strips)
    def _(distance):
        pl.semaphore_signal(
            barrier,
            inc=1,
            device_id={"strip": lax.rem(me + distance, strips)},
            device_id_type=MESH,
        )

    fetch = pltpu.make_async_copy(data, wide.at[:, ry : ry + own], local_sem)
    fetch.start()
    fetch_first.wait()
    img[0, halo : halo + own] = first[...].astype(BF)
    for side in range(2):
        at_image = slice(0, halo) if side == 0 else slice(halo + own, 2 * halo + own)
        at_data = slice(0, ry) if side == 0 else slice(ry + own, 2 * ry + own)

        @pl.when(jnp.logical_not(has[side]))
        def _():
            for step in range(ITERS):
                img[step, at_image] = jnp.zeros((halo, length_x, length_z), BF)
            wide[:, at_data] = jnp.zeros((views, ry, length_x, length_z), BF)

    def image_copy(step, side):
        if side == 0:
            source, target = pl.ds(halo, halo), pl.ds(halo + own, halo)
        else:
            source, target = pl.ds(own, halo), pl.ds(0, halo)
        return pltpu.make_async_remote_copy(
            src_ref=img.at[step, source],
            dst_ref=img.at[step, target],
            send_sem=img_send.at[step, side],
            recv_sem=img_recv.at[step, 1 - side],
            device_id={"strip": peer[side]},
            device_id_type=MESH,
        )

    def data_copy(view, side):
        if side == 0:
            source, target = pl.ds(0, ry), pl.ds(ry + own, ry)
        else:
            source, target = pl.ds(own - ry, ry), pl.ds(0, ry)
        return pltpu.make_async_remote_copy(
            src_ref=data.at[view, source],
            dst_ref=wide.at[view, target],
            send_sem=data_send.at[side, view],
            recv_sem=data_recv.at[1 - side, view],
            device_id={"strip": peer[side]},
            device_id_type=MESH,
        )

    def sum_copy(distance):
        return pltpu.make_async_remote_copy(
            src_ref=mine,
            dst_ref=parts.at[me],
            send_sem=sum_send.at[distance],
            recv_sem=sum_recv.at[distance],
            device_id={"strip": lax.rem(me + distance, strips)},
            device_id_type=MESH,
        )

    pl.semaphore_wait(barrier, strips - 1)
    for side in range(2):
        @pl.when(has[side])
        def _():
            image_copy(0, side).start()

    for view in range(min(AHEAD, views)):
        for side in range(2):
            @pl.when(has[side])
            def _():
                data_copy(view, side).start()

    fetch.wait()

    @pl.loop(0, views)
    def _(view):
        def add(chunk, total):
            at = pl.ds(pl.multiple_of(chunk * 32, 32), 32)
            for o in range(own):
                total = total + wide[view, ry + o, at, :].astype(F32)
            return total

        total = lax.fori_loop(
            0, length_x // 32, add, jnp.zeros((32, length_z), F32), unroll=2
        )
        mine[pl.ds(view, 1), :] = jnp.sum(total, axis=0, keepdims=True)

    @pl.loop(1, strips)
    def _(distance):
        sum_copy(distance).start()

    parts[me] = mine[...]

    @pl.loop(0, views)
    def _(view):
        taps_x, taps_z = normalised(nx, view), normalised(nz, view)
        for chunk in range(0, length_x, 64):
            at = pl.ds(chunk, 64)
            ax[view, at] = band(taps_x, length_x, rx, chunk, 64, False)
            axt[view, at] = band(taps_x, length_x, rx, chunk, 64, True)
        for chunk in range(0, length_z, 64):
            at = pl.ds(chunk, 64)
            bz[view, at] = band(taps_z, length_z, rz, chunk, 64, True)
            bzt[view, at] = band(taps_z, length_z, rz, chunk, 64, False)

    @pl.loop(1, strips)
    def _(distance):
        sum_copy(distance).wait()

    totals = jnp.sum(jnp.sum(parts[...], axis=0), axis=1, keepdims=True)
    weights = jnp.sum(totals, axis=0, keepdims=True) / (views * totals)
    mine[...] = jnp.broadcast_to(weights, mine.shape)

    def y_then_z(source, count, taps, mirror, matrix):
        @pl.loop(0, length_x // BLOCK, unroll=2)
        def _(block):
            starts = [
                pl.multiple_of(block * BLOCK + c, CHUNK) for c in range(0, BLOCK, CHUNK)
            ]
            pieces = []
            for start in starts:
                rows = [source(j, pl.ds(start, CHUNK)) for j in range(count)]
                pieces += [p.astype(BF) for p in along_y(rows, taps, mirror)]
            outs = len(pieces) // len(starts)
            result = dot(jnp.concatenate(pieces, axis=0), matrix).astype(BF)
            for index in range(len(pieces)):
                at = pl.ds(starts[index // outs], CHUNK)
                half[index % outs, at, :] = result[index * CHUNK : (index + 1) * CHUNK]

    for step in range(ITERS):
        for side in range(2):
            @pl.when(has[side])
            def _():
                image_copy(step, 1 - side).wait_recv()

        acc[...] = jnp.zeros_like(acc)
        kind = KINDS[step]

        @pl.loop(0, views)
        def _(view):
            taps = [
                jnp.full((CHUNK, length_z), tap, F32).astype(kind)
                for tap in normalised(ny, view)
            ]
            weight = mine[pl.ds(view, 1), :]

            y_then_z(
                lambda j, at: img[step, j, at, :].astype(kind),
                own + 2 * halo, taps, False, bz[view],
            )

            if step == 0:
                for side in range(2):
                    @pl.when(has[side])
                    def _():
                        data_copy(view, 1 - side).wait_recv()
                        data_copy(view, side).wait_send()

                        @pl.when(view < views - AHEAD)
                        def _():
                            data_copy(view + AHEAD, side).start()

            for o in range(inner):
                blurred = dot(ax[view], half[o])
                scaled = wide[view, o].astype(F32) * weight
                ratio[o] = (scaled * pl.reciprocal(blurred, approx=True)).astype(BF)

            y_then_z(
                lambda j, at: ratio[j, at, :].astype(kind), inner, taps, True, bzt[view]
            )

            for o in range(own):
                acc[o] += jnp.log(dot(axt[view], half[o]))

        before = first if step == 0 else out
        out[...] = before[...] * jnp.exp(acc[...] * (1.0 / views))
        if step < ITERS - 1:
            img[step + 1, halo : halo + own] = out[...].astype(BF)
            for side in range(2):
                @pl.when(has[side])
                def _():
                    image_copy(step + 1, side).start()

    for side in range(2):
        @pl.when(has[side])
        def _():
            for step in range(ITERS):
                image_copy(step, side).wait_send()


def local(strips, estimate, views_data, kernel_x, kernel_y, kernel_z):
    views, own, length_x, length_z = views_data.shape
    ry = (kernel_y.shape[1] - 1) // 2
    inner = own + 2 * ry
    smem = pl.BlockSpec(memory_space=pltpu.SMEM)
    vmem = pl.BlockSpec(memory_space=pltpu.VMEM)
    hbm = pl.BlockSpec(memory_space=pl.ANY)
    plane = (length_x, length_z)
    flops = ITERS * views * (inner + own) * 2 * length_x * length_z * (length_x + length_z)
    return pl.pallas_call(
        functools.partial(kernel, strips),
        out_shape=jax.ShapeDtypeStruct(estimate.shape, F32),
        in_specs=[smem, smem, smem, hbm, hbm],
        out_specs=vmem,
        scratch_shapes=[
            pltpu.VMEM((ITERS, own + 4 * ry) + plane, BF),
            pltpu.VMEM((views, inner) + plane, BF),
            pltpu.VMEM((views, length_x, length_x), BF),
            pltpu.VMEM((views, length_x, length_x), BF),
            pltpu.VMEM((views, length_z, length_z), BF),
            pltpu.VMEM((views, length_z, length_z), BF),
            pltpu.VMEM((inner,) + plane, BF),
            pltpu.VMEM((inner,) + plane, BF),
            pltpu.VMEM((own,) + plane, F32),
            pltpu.VMEM((own,) + plane, F32),
            pltpu.VMEM((views, length_z), F32),
            pltpu.VMEM((strips, views, length_z), F32),
            pltpu.SemaphoreType.DMA,
            pltpu.SemaphoreType.DMA,
            pltpu.SemaphoreType.DMA((ITERS, 2)),
            pltpu.SemaphoreType.DMA((ITERS, 2)),
            pltpu.SemaphoreType.DMA((2, views)),
            pltpu.SemaphoreType.DMA((2, views)),
            pltpu.SemaphoreType.DMA((strips,)),
            pltpu.SemaphoreType.DMA((strips,)),
        ],
        compiler_params=pltpu.CompilerParams(
            collective_id=0, has_side_effects=True, vmem_limit_bytes=44 * 1024 * 1024
        ),
        cost_estimate=pl.CostEstimate(
            flops=flops, bytes_accessed=8 * 1024 * 1024, transcendentals=0
        ),
    )(kernel_x, kernel_y, kernel_z, estimate, views_data)


def solution(mesh):
    placed = (
        P(("blocks", "strip"), None, None),
        P(None, ("blocks", "strip"), None, None),
        P(),
        P(),
        P(),
    )
    return jax.shard_map(
        functools.partial(local, mesh.shape["strip"]),
        mesh=mesh,
        in_specs=placed,
        out_specs=P(("blocks", "strip"), None, None),
        check_vma=False,
    )
```

time: 135 us -> 114 us (0.84)
  the two profiles are of different devices: /device:TPU:1 before, /device:TPU:11 now
where the time goes in v1:
time: 114 us
  Pallas kernels  107 us (94%)
  local copies, waits for them, and re-layouts  6.44 us (6%)
    pallas_call x1, Pallas kernels, local(): pl.pallas_call(functools.partial(kernel, strips), out_shape=jax.ShapeDtyp...  107 us
    unnamed x11, local copies, waits for them, and re-layouts  6.44 us

profile of v1, /device:TPU:11, one launch (start us, length us, event | category | flops | bytes accessed | tf_op | source)
XLA Modules:
  0.0 113.7 jit_solution(484606844872320054)
XLA Ops:
  0.0 0.0 copy-start
  0.0 2.2 %copy-done = bf16[8,4,256,256]{3,2,1,0:T(8,128)(2,1)S(1)} copy-done((bf16[8,4,256,256]{3,2,1,0:T(8,128)(2,1)S(1)}, bf16[8,4,256,256]{3,2,1,0:T(8,128)(2,1)}, u32[]{:S(2)}) %copy-start) | copy-done | bytes 4194328
  2.2 0.0 copy-start.1
  2.2 1.2 %copy-done.1 = f32[4,256,256]{2,1,0:T(8,128)S(1)} copy-done((f32[4,256,256]{2,1,0:T(8,128)S(1)}, f32[4,256,256]{2,1,0:T(8,128)}, u32[]{:S(2)}) %copy-start.1) | copy-done | bytes 1048600
  3.4 0.0 copy-start.2
  3.4 0.7 copy-done.2
  4.1 0.0 copy-start.3
  4.1 0.7 copy-done.3
  4.8 0.0 copy-start.4
  4.8 0.7 copy-done.4
  5.5 107.3 %shard_map.55 = f32[4,256,256]{2,1,0:T(8,128)S(1)} custom-call(f32[8,9]{1,0:T(8,128)S(1)} %copy-done.2, f32[8,5]{1,0:T(8,128)S(1)} %copy-done.3, f32[8,9]{1,0:T(8,128)S(1)} %copy-done.4, f32[4,256,256]{2,1,0:T(8,128)S(1)} %copy-done.1, bf16[8,4,256,256]{3,2,1,0:T(8,128)(2,1)S(1)} %copy-done), custom_call_target="tpu_custom_call" | custom-call | flops 12884901888 | bytes 8388608 | tf_op jit(solution)/shard_map/pallas_call | solution.py:276
  112.8 1.0 copy.7
Async XLA Ops:
  0.0 2.2 %copy-start = (bf16[8,4,256,256]{3,2,1,0:T(8,128)(2,1)S(1)}, bf16[8,4,256,256]{3,2,1,0:T(8,128)(2,1)}, u32[]{:S(2)}) copy-start(bf16[8,4,256,256]{3,2,1,0:T(8,128)(2,1)} %data.1) | copy-start | bytes 12582916
  2.2 1.2 %copy-start.1 = (f32[4,256,256]{2,1,0:T(8,128)S(1)}, f32[4,256,256]{2,1,0:T(8,128)}, u32[]{:S(2)}) copy-start(f32[4,256,256]{2,1,0:T(8,128)} %est.1) | copy-start | bytes 3145732
  3.4 0.7 copy-start.2
  4.1 0.7 copy-start.3
  4.8 0.7 copy-start.4

commit v2 on v1

--- a/solution.py
+++ b/solution.py
@@ -10,11 +10,11 @@
 ITERS = 2
 CHUNK = 16
 BLOCK = 64
-AHEAD = 2
+FIRST = 2
+AHEAD = 5
 MESH = pl.DeviceIdType.MESH
 BF = jnp.bfloat16
 F32 = jnp.float32
-KINDS = (F32, BF)
 
 
 def normalised(taps_ref, view):
@@ -56,7 +56,7 @@
 
 def kernel(
     strips, nx, ny, nz, est, data, out,
-    img, wide, ax, axt, bz, bzt, half, ratio, acc, first, mine, parts,
+    img, wide, ax, axt, bz, bzt, half, ratio, saved, acc, first, mine, parts,
     local_sem, est_sem, img_send, img_recv, data_send, data_recv, sum_send, sum_recv,
 ):
     views, own, length_x, length_z = data.shape
@@ -96,19 +96,32 @@
                 img[step, at_image] = jnp.zeros((halo, length_x, length_z), BF)
             wide[:, at_data] = jnp.zeros((views, ry, length_x, length_z), BF)
 
-    def image_copy(step, side):
+    def image_copy(step, part, side):
         if side == 0:
-            source, target = pl.ds(halo, halo), pl.ds(halo + own, halo)
+            source, target = halo + part * ry, halo + own + part * ry
         else:
-            source, target = pl.ds(own, halo), pl.ds(0, halo)
+            source, target = halo + own - (1 + part) * ry, halo - (1 + part) * ry
         return pltpu.make_async_remote_copy(
-            src_ref=img.at[step, source],
-            dst_ref=img.at[step, target],
-            send_sem=img_send.at[step, side],
-            recv_sem=img_recv.at[step, 1 - side],
+            src_ref=img.at[step, pl.ds(source, ry)],
+            dst_ref=img.at[step, pl.ds(target, ry)],
+            send_sem=img_send.at[step, part, side],
+            recv_sem=img_recv.at[step, part, 1 - side],
             device_id={"strip": peer[side]},
             device_id_type=MESH,
         )
+
+    def send_image(step):
+        for part in range(2):
+            for side in range(2):
+                @pl.when(has[side])
+                def _():
+                    image_copy(step, part, side).start()
+
+    def wait_image(step, part):
+        for side in range(2):
+            @pl.when(has[side])
+            def _():
+                image_copy(step, part, 1 - side).wait_recv()
 
     def data_copy(view, side):
         if side == 0:
@@ -135,12 +148,9 @@
         )
 
     pl.semaphore_wait(barrier, strips - 1)
-    for side in range(2):
-        @pl.when(has[side])
-        def _():
-            image_copy(0, side).start()
-
-    for view in range(min(AHEAD, views)):
+    send_image(0)
+
+    for view in range(min(FIRST, views)):
         for side in range(2):
             @pl.when(has[side])
             def _():
@@ -183,11 +193,31 @@
     def _(distance):
         sum_copy(distance).wait()
 
+    for view in range(min(FIRST, views), min(AHEAD, views)):
+        for side in range(2):
+            @pl.when(has[side])
+            def _():
+                data_copy(view, side).start()
+
     totals = jnp.sum(jnp.sum(parts[...], axis=0), axis=1, keepdims=True)
     weights = jnp.sum(totals, axis=0, keepdims=True) / (views * totals)
     mine[...] = jnp.broadcast_to(weights, mine.shape)
 
-    def y_then_z(source, count, taps, mirror, matrix):
+    def splat(view, kind):
+        return [
+            jnp.full((CHUNK, length_z), tap, F32).astype(kind)
+            for tap in normalised(ny, view)
+        ]
+
+    def y_only(source, count, taps, mirror):
+        @pl.loop(0, length_x // CHUNK, unroll=2)
+        def _(chunk):
+            at = pl.ds(pl.multiple_of(chunk * CHUNK, CHUNK), CHUNK)
+            rows = [source(j, at).astype(F32) for j in range(count)]
+            for o, value in enumerate(along_y(rows, taps, mirror)):
+                half[o, at, :] = value.astype(BF)
+
+    def y_then_z(runs, taps, mirror, matrix):
         @pl.loop(0, length_x // BLOCK, unroll=2)
         def _(block):
             starts = [
@@ -195,73 +225,89 @@
             ]
             pieces = []
             for start in starts:
-                rows = [source(j, pl.ds(start, CHUNK)) for j in range(count)]
-                pieces += [p.astype(BF) for p in along_y(rows, taps, mirror)]
+                for run in runs:
+                    rows = [source(pl.ds(start, CHUNK)) for source in run]
+                    pieces += along_y(rows, taps, mirror)
             outs = len(pieces) // len(starts)
             result = dot(jnp.concatenate(pieces, axis=0), matrix).astype(BF)
             for index in range(len(pieces)):
                 at = pl.ds(starts[index // outs], CHUNK)
                 half[index % outs, at, :] = result[index * CHUNK : (index + 1) * CHUNK]
 
-    for step in range(ITERS):
+    def ratio_of(view, o, blurred):
+        scaled = wide[view, o].astype(F32) * mine[pl.ds(view, 1), :]
+        return (scaled * pl.reciprocal(blurred, approx=True)).astype(BF)
+
+    def image_row(step, j):
+        return lambda at: img[step, j, at, :]
+
+    wait_image(0, 0)
+    wait_image(0, 1)
+    acc[...] = jnp.zeros_like(acc)
+
+    @pl.loop(0, views)
+    def _(view):
+        taps = splat(view, F32)
+        y_only(lambda j, at: img[0, j, at, :], own + 2 * halo, taps, False)
         for side in range(2):
             @pl.when(has[side])
             def _():
-                image_copy(step, 1 - side).wait_recv()
-
+                data_copy(view, 1 - side).wait_recv()
+                data_copy(view, side).wait_send()
+
+                @pl.when(view < views - AHEAD)
+                def _():
+                    data_copy(view + AHEAD, side).start()
+
+        for o in range(inner):
+            second = dot(ax[view], half[o]).astype(BF)
+            ratio[o] = ratio_of(view, o, dot(second, bz[view]))
+        y_only(lambda j, at: ratio[j, at, :], inner, taps, True)
+        for o in range(own):
+            second = dot(axt[view], half[o]).astype(BF)
+            acc[o] += jnp.log(dot(second, bzt[view]))
+
+    out[...] = first[...] * jnp.exp(acc[...] * (1.0 / views))
+
+    for step in range(1, ITERS):
+        img[step, halo : halo + own] = out[...].astype(BF)
+        send_image(step)
         acc[...] = jnp.zeros_like(acc)
-        kind = KINDS[step]
+        wait_image(step, 0)
 
         @pl.loop(0, views)
         def _(view):
-            taps = [
-                jnp.full((CHUNK, length_z), tap, F32).astype(kind)
-                for tap in normalised(ny, view)
-            ]
-            weight = mine[pl.ds(view, 1), :]
-
-            y_then_z(
-                lambda j, at: img[step, j, at, :].astype(kind),
-                own + 2 * halo, taps, False, bz[view],
-            )
-
-            if step == 0:
-                for side in range(2):
-                    @pl.when(has[side])
-                    def _():
-                        data_copy(view, 1 - side).wait_recv()
-                        data_copy(view, side).wait_send()
-
-                        @pl.when(view < views - AHEAD)
-                        def _():
-                            data_copy(view + AHEAD, side).start()
-
-            for o in range(inner):
-                blurred = dot(ax[view], half[o])
-                scaled = wide[view, o].astype(F32) * weight
-                ratio[o] = (scaled * pl.reciprocal(blurred, approx=True)).astype(BF)
-
-            y_then_z(
-                lambda j, at: ratio[j, at, :].astype(kind), inner, taps, True, bzt[view]
-            )
-
+            run = [image_row(step, j) for j in range(ry, inner + ry)]
+            y_then_z([run], splat(view, BF), False, bz[view])
+            for o in range(own):
+                saved[view, o] = ratio_of(view, ry + o, dot(ax[view], half[o]))
+
+        wait_image(step, 1)
+
+        @pl.loop(0, views)
+        def _(view):
+            taps = splat(view, BF)
+            low = [image_row(step, j) for j in range(3 * ry)]
+            high = [image_row(step, j + ry + own) for j in range(3 * ry)]
+            y_then_z([low, high], taps, False, bz[view])
+            for o in range(2 * ry):
+                row = o if o < ry else o + own
+                ratio[o] = ratio_of(view, row, dot(ax[view], half[o]))
+            run = [(lambda at, o=o: ratio[o, at, :]) for o in range(ry)]
+            run += [(lambda at, o=o: saved[view, o, at, :]) for o in range(own)]
+            run += [(lambda at, o=o: ratio[o, at, :]) for o in range(ry, 2 * ry)]
+            y_then_z([run], taps, True, bzt[view])
             for o in range(own):
                 acc[o] += jnp.log(dot(axt[view], half[o]))
 
-        before = first if step == 0 else out
-        out[...] = before[...] * jnp.exp(acc[...] * (1.0 / views))
-        if step < ITERS - 1:
-            img[step + 1, halo : halo + own] = out[...].astype(BF)
-            for side in range(2):
-                @pl.when(has[side])
-                def _():
-                    image_copy(step + 1, side).start()
+        out[...] = out[...] * jnp.exp(acc[...] * (1.0 / views))
 
     for side in range(2):
         @pl.when(has[side])
         def _():
             for step in range(ITERS):
-                image_copy(step, side).wait_send()
+                for part in range(2):
+                    image_copy(step, part, side).wait_send()
 
 
 def local(strips, estimate, views_data, kernel_x, kernel_y, kernel_z):
@@ -270,7 +316,7 @@
     inner = own + 2 * ry
     smem = pl.BlockSpec(memory_space=pltpu.SMEM)
     vmem = pl.BlockSpec(memory_space=pltpu.VMEM)
-    hbm = pl.BlockSpec(memory_space=pl.ANY)
+    hbm = pl.BlockSpec(memory_space=pltpu.HBM)
     plane = (length_x, length_z)
     flops = ITERS * views * (inner + own) * 2 * length_x * length_z * (length_x + length_z)
     return pl.pallas_call(
@@ -287,14 +333,15 @@
             pltpu.VMEM((views, length_z, length_z), BF),
             pltpu.VMEM((inner,) + plane, BF),
             pltpu.VMEM((inner,) + plane, BF),
+            pltpu.VMEM((views, own) + plane, BF),
             pltpu.VMEM((own,) + plane, F32),
             pltpu.VMEM((own,) + plane, F32),
             pltpu.VMEM((views, length_z), F32),
             pltpu.VMEM((strips, views, length_z), F32),
             pltpu.SemaphoreType.DMA,
             pltpu.SemaphoreType.DMA,
-            pltpu.SemaphoreType.DMA((ITERS, 2)),
-            pltpu.SemaphoreType.DMA((ITERS, 2)),
+            pltpu.SemaphoreType.DMA((ITERS, 2, 2)),
+            pltpu.SemaphoreType.DMA((ITERS, 2, 2)),
             pltpu.SemaphoreType.DMA((2, views)),
             pltpu.SemaphoreType.DMA((2, views)),
             pltpu.SemaphoreType.DMA((strips,)),

time: 114 us -> 107 us (0.939)
  the two profiles are of different devices: /device:TPU:11 before, /device:TPU:1 now
where the time goes in v2:
time: 107 us
  Pallas kernels  101 us (94%)
  local copies, waits for them, and re-layouts  6.44 us (6%)
    pallas_call x1, Pallas kernels, local(): pl.pallas_call(functools.partial(kernel, strips), out_shape=jax.ShapeDtyp...  101 us
    unnamed x11, local copies, waits for them, and re-layouts  6.44 us

profile of v2, /device:TPU:1, one launch (start us, length us, event | category | flops | bytes accessed | tf_op | source)
XLA Modules:
  0.0 107.2 jit_solution(14509030976923583623)
XLA Ops:
  0.0 0.0 copy-start
  0.0 2.2 %copy-done = bf16[8,4,256,256]{3,2,1,0:T(8,128)(2,1)S(1)} copy-done((bf16[8,4,256,256]{3,2,1,0:T(8,128)(2,1)S(1)}, bf16[8,4,256,256]{3,2,1,0:T(8,128)(2,1)}, u32[]{:S(2)}) %copy-start) | copy-done | bytes 4194328
  2.2 0.0 copy-start.1
  2.2 1.2 %copy-done.1 = f32[4,256,256]{2,1,0:T(8,128)S(1)} copy-done((f32[4,256,256]{2,1,0:T(8,128)S(1)}, f32[4,256,256]{2,1,0:T(8,128)}, u32[]{:S(2)}) %copy-start.1) | copy-done | bytes 1048600
  3.4 0.0 copy-start.2
  3.4 0.7 copy-done.2
  4.1 0.0 copy-start.3
  4.1 0.7 copy-done.3
  4.8 0.0 copy-start.4
  4.8 0.7 copy-done.4
  5.5 100.7 %shard_map.55 = f32[4,256,256]{2,1,0:T(8,128)S(1)} custom-call(f32[8,9]{1,0:T(8,128)S(1)} %copy-done.2, f32[8,5]{1,0:T(8,128)S(1)} %copy-done.3, f32[8,9]{1,0:T(8,128)S(1)} %copy-done.4, f32[4,256,256]{2,1,0:T(8,128)S(1)} %copy-done.1, bf16[8,4,256,256]{3,2,1,0:T(8,128)(2,1)S(1)} %copy-done), custom_call_target="tpu_custom_call" | custom-call | flops 12884901888 | bytes 8388608 | tf_op jit(solution)/shard_map/pallas_call | solution.py:322
  106.2 1.0 copy.7
Async XLA Ops:
  0.0 2.2 %copy-start = (bf16[8,4,256,256]{3,2,1,0:T(8,128)(2,1)S(1)}, bf16[8,4,256,256]{3,2,1,0:T(8,128)(2,1)}, u32[]{:S(2)}) copy-start(bf16[8,4,256,256]{3,2,1,0:T(8,128)(2,1)} %data.1) | copy-start | bytes 12582916
  2.2 1.2 %copy-start.1 = (f32[4,256,256]{2,1,0:T(8,128)S(1)}, f32[4,256,256]{2,1,0:T(8,128)}, u32[]{:S(2)}) copy-start(f32[4,256,256]{2,1,0:T(8,128)} %est.1) | copy-start | bytes 3145732
  3.4 0.7 copy-start.2
  4.1 0.7 copy-start.3
  4.8 0.7 copy-start.4

commit v3 on v2

--- a/solution.py
+++ b/solution.py
@@ -218,7 +218,7 @@
                 half[o, at, :] = value.astype(BF)
 
     def y_then_z(runs, taps, mirror, matrix):
-        @pl.loop(0, length_x // BLOCK, unroll=2)
+        @pl.loop(0, length_x // BLOCK, unroll=4)
         def _(block):
             starts = [
                 pl.multiple_of(block * BLOCK + c, CHUNK) for c in range(0, BLOCK, CHUNK)

time: 107 us -> 101 us (0.944)
  Pallas kernels: 101 us -> 94.7 us
    pallas_call x1, Pallas kernels: 101 us -> 94.7 us  [local(): pl.pallas_call(functools.partial(kernel, strips), out_shape=jax.ShapeDtyp...]
where the time goes in v3:
time: 101 us
  Pallas kernels  94.7 us (94%)
  local copies, waits for them, and re-layouts  6.44 us (6%)
    pallas_call x1, Pallas kernels, local(): pl.pallas_call(functools.partial(kernel, strips), out_shape=jax.ShapeDtyp...  94.7 us
    unnamed x11, local copies, waits for them, and re-layouts  6.44 us

profile of v3, /device:TPU:1, one launch (start us, length us, event | category | flops | bytes accessed | tf_op | source)
XLA Modules:
  0.0 101.2 jit_solution(8626627198605604919)
XLA Ops:
  0.0 0.0 copy-start
  0.0 2.2 %copy-done = bf16[8,4,256,256]{3,2,1,0:T(8,128)(2,1)S(1)} copy-done((bf16[8,4,256,256]{3,2,1,0:T(8,128)(2,1)S(1)}, bf16[8,4,256,256]{3,2,1,0:T(8,128)(2,1)}, u32[]{:S(2)}) %copy-start) | copy-done | bytes 4194328
  2.2 0.0 copy-start.1
  2.2 1.2 %copy-done.1 = f32[4,256,256]{2,1,0:T(8,128)S(1)} copy-done((f32[4,256,256]{2,1,0:T(8,128)S(1)}, f32[4,256,256]{2,1,0:T(8,128)}, u32[]{:S(2)}) %copy-start.1) | copy-done | bytes 1048600
  3.4 0.0 copy-start.2
  3.4 0.7 copy-done.2
  4.1 0.0 copy-start.3
  4.1 0.7 copy-done.3
  4.8 0.0 copy-start.4
  4.8 0.7 copy-done.4
  5.5 94.7 %shard_map.55 = f32[4,256,256]{2,1,0:T(8,128)S(1)} custom-call(f32[8,9]{1,0:T(8,128)S(1)} %copy-done.2, f32[8,5]{1,0:T(8,128)S(1)} %copy-done.3, f32[8,9]{1,0:T(8,128)S(1)} %copy-done.4, f32[4,256,256]{2,1,0:T(8,128)S(1)} %copy-done.1, bf16[8,4,256,256]{3,2,1,0:T(8,128)(2,1)S(1)} %copy-done), custom_call_target="tpu_custom_call" | custom-call | flops 12884901888 | bytes 8388608 | tf_op jit(solution)/shard_map/pallas_call | solution.py:322
  100.2 1.0 copy.7
Async XLA Ops:
  0.0 2.2 %copy-start = (bf16[8,4,256,256]{3,2,1,0:T(8,128)(2,1)S(1)}, bf16[8,4,256,256]{3,2,1,0:T(8,128)(2,1)}, u32[]{:S(2)}) copy-start(bf16[8,4,256,256]{3,2,1,0:T(8,128)(2,1)} %data.1) | copy-start | bytes 12582916
  2.2 1.2 %copy-start.1 = (f32[4,256,256]{2,1,0:T(8,128)S(1)}, f32[4,256,256]{2,1,0:T(8,128)}, u32[]{:S(2)}) copy-start(f32[4,256,256]{2,1,0:T(8,128)} %est.1) | copy-start | bytes 3145732
  3.4 0.7 copy-start.2
  4.1 0.7 copy-start.3
  4.8 0.7 copy-start.4
